TPU v7x, 256 devices: a whole 4x4x8 slice. The times are simulated.
256 devices in a mesh: band: 64 (over z_lo, y, x), dom: 4 (over z_hi, core).
Axes of the slice: x: 4, y: 4, z: 8 (z_hi: 2, z_lo: 4; z = z_hi * 4 + z_lo), core: 2. Of those that a mesh axis runs over, the one named last changes fastest.
Arguments:
- orbitals: float32 [128, 128, 16, 128], P('band', 'dom'), may hold values from -6 to 6
- potential: float32 [128, 16, 128], P('dom'), may hold values from -1 to 0
- subspace: float32 [128, 128], P('band'), may hold values from -0.4 to 2.4, as said below
Outputs:
- rotated: float32 [128, 262144], P(None, ('dom', 'band'))
Inputs may be any that keep to these rules, and one draw needn't show every extreme that they name: `subspace`: diagonal entries between 0.7 and 2.3, off-diagonal entries small and independent.
All inputs are finite; a program needn't handle non-finite values.
Results may differ from a plain program's by a relative error of at most 0.00012.
Values sent between devices are 32-bit elements; how exact they have to be, the bound alone decides.
A program may use at most 128 MiB of HBM per device.

v0:
```python
import functools
import math

import jax
import jax.numpy as jnp
from jax import lax
from jax.experimental import pallas as pl
from jax.experimental.pallas import tpu as pltpu
from jax.sharding import PartitionSpec as P

DEG = 3
REACH = 6
MESH = pl.DeviceIdType.MESH

upper_edge = 10.7
lower_edge = 1.5
bottom_edge = -1.0


def stencil_weights():
    factor_square = math.factorial(6) ** 2
    side_weights = []
    for offset in range(1, 7):
        side_weights.append(
            2.0
            * (-1.0) ** (offset + 1)
            * factor_square
            / (offset * offset * math.factorial(6 - offset) * math.factorial(6 + offset))
        )
    center_weight = -2.0 * sum(side_weights)
    return (center_weight, side_weights)


def filter_scalars(pass_count):
    half_width = (upper_edge - lower_edge) / 2.0
    sigma_now = half_width / (bottom_edge - (upper_edge + lower_edge) / 2.0)
    gamma_value = 2.0 / sigma_now
    scalars = [(sigma_now / half_width, 0.0)]
    for pass_index in range(pass_count - 1):
        sigma_next = 1.0 / (gamma_value - sigma_now)
        scalars.append((2.0 * sigma_next / half_width, sigma_now * sigma_next))
        sigma_now = sigma_next
    return scalars


def two_parts(values):
    high = values.astype(jnp.bfloat16)
    return high, (values - high.astype(jnp.float32)).astype(jnp.bfloat16)


def lane_matrix():
    rows = lax.broadcasted_iota(jnp.int32, (128, 128), 0)
    columns = lax.broadcasted_iota(jnp.int32, (128, 128), 1)
    apart = jnp.abs(rows - columns)
    apart = jnp.minimum(apart, 128 - apart)
    matrix = jnp.zeros((128, 128), jnp.float32)
    for k, w in enumerate(stencil_weights()[1], 1):
        matrix = jnp.where(apart == k, jnp.float32(w), matrix)
    high, low = two_parts(matrix)
    return jnp.concatenate([high, high, low], axis=0)


def row_weights():
    side = stencil_weights()[1]
    weight = lambda k: side[k - 1] if 1 <= k <= REACH else 0.0
    rows = lax.broadcasted_iota(jnp.int32, (8, 128), 0)
    cyclic, negacyclic = {}, {}
    for r in range(1, 8):
        cyclic[r] = 0.5 * (weight(r) + weight(8 - r))
        if r != 4:
            w = 0.5 * (weight(r) - weight(8 - r))
            negacyclic[r] = jnp.where(rows >= r, jnp.float32(w), jnp.float32(-w))
    return cyclic, negacyclic


def filtered_block(window, pot, before, scale, weight, lanes, cyclic, negacyclic):
    center_weight, side = stencil_weights()
    n = window.shape[0] - 2 * REACH
    mid = window[REACH : REACH + n]
    high, low = two_parts(mid.reshape(n * 16, 128))
    total = jnp.dot(
        jnp.concatenate([high, low, high], axis=1), lanes, preferred_element_type=jnp.float32
    ).reshape(n, 2, 8, 128)
    for k in range(1, REACH + 1):
        beside = window[REACH + k : REACH + k + n] + window[REACH - k : REACH - k + n]
        total = total + side[k - 1] * beside
    both, apart = mid[:, 0] + mid[:, 1], mid[:, 0] - mid[:, 1]
    even = cyclic[4] * pltpu.roll(both, 4, 1)
    for r in range(1, 4):
        even = even + cyclic[r] * (pltpu.roll(both, r, 1) + pltpu.roll(both, 8 - r, 1))
    odd = None
    for r, w in negacyclic.items():
        term = w * pltpu.roll(apart, r, 1)
        odd = term if odd is None else odd + term
    diag = (-1.5 * center_weight - (upper_edge + lower_edge) / 2.0) * scale
    results = []
    for at, rows in enumerate((even + odd, even - odd)):
        result = (pot[:, at] * scale + diag) * mid[:, at]
        result = result + (-0.5 * scale) * (total[:, at] + rows)
        if before is not None:
            result = result - weight * before[:, at]
        results.append(result)
    return results


def filter_kernel(
    bands, doms, orb, pot, sub, recv, rows, p0, p1, p2, out, pot_v,
    near_send, near_recv, far_send, far_recv, pot_send, pot_recv,
    move_sem, all_send, all_recv, row_send, row_recv,
):
    orbs, planes = orb.shape[0], orb.shape[1]
    band, dom = lax.axis_index("band"), lax.axis_index("dom")
    core, half = lax.rem(dom, 2), lax.div(dom, 2)
    side = 4
    zl, y, x = lax.div(band, side * side), lax.rem(lax.div(band, side), side), lax.rem(band, side)
    sibling = {"dom": dom + 1 - 2 * core}
    across = {"dom": 2 * (1 - half) + 1 - core}
    scalars = filter_scalars(DEG)
    buffers = (p0, p1, p2, out)
    rims = tuple(REACH * (DEG - level) for level in range(DEG + 1))
    deep, pot_rim = rims[0], rims[1]
    step = 4

    load = pltpu.make_async_copy(orb, p0.at[:, pl.ds(deep, planes)], move_sem.at[0])
    load.start()
    load_pot = pltpu.make_async_copy(pot, pot_v.at[pl.ds(pot_rim, planes)], move_sem.at[1])
    load_pot.start()

    def neighbour(i):
        dz, dy, dx = lax.rem(i, side), lax.rem(lax.div(i, side), side), lax.div(i, side * side)
        return (
            lax.rem(zl + dz, side) * side * side + lax.rem(y + dy, side) * side + lax.rem(x + dx, side)
        )

    barrier = pltpu.get_barrier_semaphore()
    for peer in (sibling, across):
        pl.semaphore_signal(barrier, inc=1, device_id=peer, device_id_type=MESH)

    def greet(i, c):
        pl.semaphore_signal(
            barrier, inc=1, device_id={"band": neighbour(i)}, device_id_type=MESH
        )
        return c

    lax.fori_loop(1, bands, greet, 0)
    lanes = lane_matrix()
    cyclic, negacyclic = row_weights()
    pl.semaphore_wait(barrier, bands + 1)

    def remote(src, dst, send_sem, recv_sem, peer):
        return pltpu.make_async_remote_copy(
            src_ref=src, dst_ref=dst, send_sem=send_sem, recv_sem=recv_sem,
            device_id=peer, device_id_type=MESH,
        )

    def rim_copies(src, dst, width, sems_near, sems_far):
        inner = planes - width
        near = remote(
            src.at[pl.ds((1 - core) * inner, width)],
            dst.at[pl.ds(core * (planes + width), width)], *sems_near, sibling,
        )
        far = remote(
            src.at[pl.ds(core * inner, width)],
            dst.at[pl.ds((1 - core) * (planes + width), width)], *sems_far, across,
        )
        return near, far

    part = pot_rim // side
    pot_far = remote(
        pot.at[pl.ds(core * (planes - pot_rim) + x * part, part)],
        pot_v.at[pl.ds((1 - core) * (planes + pot_rim) + x * part, part)],
        pot_send.at[0], pot_recv.at[0], across,
    )
    pot_near = remote(
        pot.at[pl.ds((1 - core) * (planes - pot_rim), pot_rim)],
        pot_v.at[pl.ds(core * (planes + pot_rim), pot_rim)],
        pot_send.at[1], pot_recv.at[1], sibling,
    )
    pot_far.start()
    pot_near.start()
    nears, fars = [], []
    for o in range(orbs):
        near, far = rim_copies(
            orb.at[o], p0.at[o], deep,
            (near_send.at[o], near_recv.at[o]), (far_send.at[o], far_recv.at[o]),
        )
        far.start()
        near.start()
        nears.append(near)
        fars.append(far)

    own_rows = pltpu.make_async_copy(sub, rows.at[band], move_sem.at[2])
    own_rows.start()

    def send_rows(i, c):
        remote(sub, rows.at[band], row_send, row_recv, {"band": neighbour(i)}).start()
        return c

    lax.fori_loop(1, bands, send_rows, 0)

    def apply(level, o, begin, blocks):
        scale, weight = scalars[level]

        def body(i, c):
            at = begin + i * step
            before = None
            if level > 0:
                before = buffers[level - 1][o, pl.ds(at + rims[level - 1], step)]
            window = buffers[level][o, pl.ds(at + rims[level] - REACH, step + 2 * REACH)]
            low, high = filtered_block(
                window, pot_v[pl.ds(at + pot_rim, step)], before, scale, weight,
                lanes, cyclic, negacyclic,
            )
            target = buffers[level + 1]
            target[o, pl.ds(at + rims[level + 1], step), 0] = low
            target[o, pl.ds(at + rims[level + 1], step), 1] = high
            return c

        lax.fori_loop(0, blocks, body, 0)

    early = [(planes + 2 * rims[level + 1] - 20) // step for level in range(DEG)]
    load.wait()
    load_pot.wait()
    pot_near.wait_recv()
    for o in range(orbs):
        nears[o].wait_recv()
        for level in range(DEG):
            rim = rims[level + 1]
            apply(level, o, core * -rim + (1 - core) * (20 - rim), early[level])

    pot_far.wait_recv()
    at_far = (planes + pot_rim) * core + x * part
    passed = []
    for d in range(1, side):
        mine = pot_v.at[pl.ds(at_far, part)]
        peer = {"band": band - x + lax.rem(x + d, side)}
        copy = remote(mine, mine, pot_send.at[1 + d], pot_recv.at[1 + d], peer)
        copy.start()
        passed.append(copy)
    for copy in passed:
        copy.wait_recv()

    def spread(o):
        own = pltpu.make_async_copy(
            out.at[o, lax.div(band, 2), lax.rem(band, 2)], recv.at[band, o], move_sem.at[3 + o]
        )
        own.start()

        def send(i, c):
            peer = neighbour(i)
            remote(
                out.at[o, lax.div(peer, 2), lax.rem(peer, 2)], recv.at[band, o],
                all_send, all_recv, {"band": peer},
            ).start()
            return c

        lax.fori_loop(1, bands, send, 0)
        return own

    owns = []
    for o in range(orbs):
        fars[o].wait_recv()
        for level in range(DEG):
            rim = rims[level + 1]
            apply(level, o, core * (planes + rim - 20) - (1 - core) * rim, 20 // step)
        owns.append(spread(o))

    for copy in (*nears, *fars, pot_far, pot_near, *passed):
        copy.wait_send()
    own_rows.wait()
    for own in owns:
        own.wait()
    for ref, sem_a, sem_b in ((rows, row_send, row_recv), (recv, all_send, all_recv)):
        whole = ref.at[pl.ds(0, bands - 1)]
        pltpu.make_async_copy(whole, whole, sem_a).wait()
        pltpu.make_async_copy(whole, whole, sem_b).wait()


def rotate_kernel(recv, rows, out, recv_v, rows_v, out_v, sems):
    load = pltpu.make_async_copy(recv, recv_v, sems.at[0])
    load_rows = pltpu.make_async_copy(rows, rows_v, sems.at[1])
    load.start()
    load_rows.start()
    load_rows.wait()
    high, low = two_parts(jnp.concatenate([rows_v[:, 0], rows_v[:, 1]], axis=0).T)
    matrix = jnp.concatenate([high, high, low], axis=1)
    load.wait()
    width = 256
    stores = []
    for at in range(0, 8 * 128, width):
        columns = []
        for r in range(at // 128, (at + width) // 128):
            values = jnp.concatenate([recv_v[:, 0, r], recv_v[:, 1, r]], axis=0)
            high, low = two_parts(values)
            columns.append(jnp.concatenate([high, low, high], axis=0))
        out_v[:, pl.ds(at, width)] = jnp.dot(
            matrix, jnp.concatenate(columns, axis=1), preferred_element_type=jnp.float32
        )
        store = pltpu.make_async_copy(
            out_v.at[:, pl.ds(at, width)], out.at[:, pl.ds(at, width)], sems.at[2 + at // width]
        )
        store.start()
        stores.append(store)
    for store in stores:
        store.wait()


def per_device(bands, doms, orbitals, potential, subspace):
    orbs, planes = orbitals.shape[0], orbitals.shape[1]
    orb = orbitals.reshape(orbs, planes, 2, 8, 128)
    pot = potential.reshape(planes, 2, 8, 128)
    f32 = jnp.float32
    dma = pltpu.SemaphoreType.DMA
    anywhere = pl.BlockSpec(memory_space=pl.ANY)
    recv, rows = pl.pallas_call(
        functools.partial(filter_kernel, bands, doms),
        out_shape=(
            jax.ShapeDtypeStruct((bands, orbs, 8, 128), f32),
            jax.ShapeDtypeStruct((bands, orbs, 128), f32),
        ),
        in_specs=[anywhere] * 3,
        out_specs=(anywhere,) * 2,
        scratch_shapes=[
            *[
                pltpu.VMEM((orbs, planes + 2 * REACH * (DEG - level), 2, 8, 128), f32)
                for level in range(DEG + 1)
            ],
            pltpu.VMEM((planes + 2 * REACH * (DEG - 1), 2, 8, 128), f32),
            dma((orbs,)),
            dma((orbs,)),
            dma((orbs,)),
            dma((orbs,)),
            dma((5,)),
            dma((5,)),
            dma((3 + orbs,)),
            dma,
            dma,
            dma,
            dma,
        ],
        compiler_params=pltpu.CompilerParams(
            collective_id=0, has_side_effects=True, vmem_limit_bytes=60 * 2**20
        ),
        name="filter",
    )(orb, pot, subspace)
    return pl.pallas_call(
        rotate_kernel,
        out_shape=jax.ShapeDtypeStruct((bands * orbs, 1024), f32),
        in_specs=[anywhere] * 2,
        out_specs=anywhere,
        scratch_shapes=[
            pltpu.VMEM((bands, orbs, 8, 128), f32),
            pltpu.VMEM((bands, orbs, 128), f32),
            pltpu.VMEM((bands * orbs, 1024), f32),
            dma((6,)),
        ],
        compiler_params=pltpu.CompilerParams(vmem_limit_bytes=60 * 2**20),
        name="rotate",
    )(recv, rows)


def solution(mesh):
    in_specs = (P("band", "dom", None, None), P("dom", None, None), P("band", None))
    out_specs = P(None, ("dom", "band"))
    return jax.shard_map(
        functools.partial(per_device, mesh.shape["band"], mesh.shape["dom"]),
        mesh=mesh,
        in_specs=in_specs,
        out_specs=out_specs,
        check_vma=False,
    )
```

profile of v0, /device:TPU:1, one launch (start us, length us, event | category | flops | bytes accessed | tf_op | source)
XLA Modules:
  0.0 44.7 jit_solution(11892097259349450932)
XLA Ops:
  0.0 42.3 %filter.1 = (f32[64,2,8,128]{3,2,1,0:T(8,128)}, f32[64,2,128]{2,1,0:T(2,128)}) custom-call(f32[2,32,2,8,128]{4,3,2,1,0:T(8,128)} %bitcast.2, f32[32,2,8,128]{3,2,1,0:T(8,128)} %bitcast.3, f32[2,128]{1,0:T(2,128)} %sub.1), custom_call_target="tpu_custom_call" | custom-call | tf_op jit(solution)/shard_map/filter/pallas_call | solution.py:315
  42.3 2.4 %rotate.1 = f32[128,1024]{1,0:T(8,128)} custom-call(f32[64,2,8,128]{3,2,1,0:T(8,128)} %get-tuple-element.7.recv, f32[64,2,128]{2,1,0:T(2,128)} %get-tuple-element.8.rows), custom_call_target="tpu_custom_call" | custom-call | tf_op jit(solution)/shard_map/rotate/pallas_call | solution.py:346
where the time goes:
time: 44.8 us; the launch traced here: 44.7 us
  Pallas kernels  44.7 us (100%)
    pallas_call x1, Pallas kernels, per_device(): pl.pallas_call(functools.partial(filter_kernel, bands, doms), out_shape=(...  42.3 us
    pallas_call x1, Pallas kernels, per_device(): pl.pallas_call(rotate_kernel, out_shape=jax.ShapeDtypeStruct((bands * orb...  2.4 us

commit v1 on v0

--- a/solution.py
+++ b/solution.py
@@ -116,7 +116,7 @@
     sibling = {"dom": dom + 1 - 2 * core}
     across = {"dom": 2 * (1 - half) + 1 - core}
     scalars = filter_scalars(DEG)
-    buffers = (p0, p1, p2, out)
+    buffers = (p0, p1, p2)
     rims = tuple(REACH * (DEG - level) for level in range(DEG + 1))
     deep, pot_rim = rims[0], rims[1]
     step = 4
@@ -126,23 +126,22 @@
     load_pot = pltpu.make_async_copy(pot, pot_v.at[pl.ds(pot_rim, planes)], move_sem.at[1])
     load_pot.start()
 
-    def neighbour(i):
-        dz, dy, dx = lax.rem(i, side), lax.rem(lax.div(i, side), side), lax.div(i, side * side)
-        return (
-            lax.rem(zl + dz, side) * side * side + lax.rem(y + dy, side) * side + lax.rem(x + dx, side)
-        )
+    along_z = [lax.rem(zl + d, side) * side * side for d in range(side)]
+    along_y = [lax.rem(y + d, side) * side for d in range(side)]
+    along_x = [lax.rem(x + d, side) for d in range(side)]
+    others = [
+        along_z[dz] + along_y[dy] + along_x[dx]
+        for dx in range(side)
+        for dy in range(side)
+        for dz in range(side)
+    ][1:]
 
     barrier = pltpu.get_barrier_semaphore()
     for peer in (sibling, across):
         pl.semaphore_signal(barrier, inc=1, device_id=peer, device_id_type=MESH)
 
-    def greet(i, c):
-        pl.semaphore_signal(
-            barrier, inc=1, device_id={"band": neighbour(i)}, device_id_type=MESH
-        )
-        return c
-
-    lax.fori_loop(1, bands, greet, 0)
+    for peer in others:
+        pl.semaphore_signal(barrier, inc=1, device_id={"band": peer}, device_id_type=MESH)
     lanes = lane_matrix()
     cyclic, negacyclic = row_weights()
     pl.semaphore_wait(barrier, bands + 1)
@@ -192,11 +191,8 @@
     own_rows = pltpu.make_async_copy(sub, rows.at[band], move_sem.at[2])
     own_rows.start()
 
-    def send_rows(i, c):
-        remote(sub, rows.at[band], row_send, row_recv, {"band": neighbour(i)}).start()
-        return c
-
-    lax.fori_loop(1, bands, send_rows, 0)
+    for peer in others:
+        remote(sub, rows.at[band], row_send, row_recv, {"band": peer}).start()
 
     def apply(level, o, begin, blocks):
         scale, weight = scalars[level]
@@ -211,9 +207,12 @@
                 window, pot_v[pl.ds(at + pot_rim, step)], before, scale, weight,
                 lanes, cyclic, negacyclic,
             )
-            target = buffers[level + 1]
-            target[o, pl.ds(at + rims[level + 1], step), 0] = low
-            target[o, pl.ds(at + rims[level + 1], step), 1] = high
+            if level < DEG - 1:
+                buffers[level + 1][o, pl.ds(at + rims[level + 1], step), 0] = low
+                buffers[level + 1][o, pl.ds(at + rims[level + 1], step), 1] = high
+            else:
+                pairs = jnp.stack([low, high], axis=1)
+                out[o, pl.ds(2 * at, 2 * step)] = pairs.reshape(2 * step, 8, 128)
             return c
 
         lax.fori_loop(0, blocks, body, 0)
@@ -242,19 +241,14 @@
 
     def spread(o):
         own = pltpu.make_async_copy(
-            out.at[o, lax.div(band, 2), lax.rem(band, 2)], recv.at[band, o], move_sem.at[3 + o]
+            out.at[o, band], recv.at[band, o], move_sem.at[3 + o]
         )
         own.start()
 
-        def send(i, c):
-            peer = neighbour(i)
+        for peer in others:
             remote(
-                out.at[o, lax.div(peer, 2), lax.rem(peer, 2)], recv.at[band, o],
-                all_send, all_recv, {"band": peer},
+                out.at[o, peer], recv.at[band, o], all_send, all_recv, {"band": peer}
             ).start()
-            return c
-
-        lax.fori_loop(1, bands, send, 0)
         return own
 
     owns = []
@@ -276,15 +270,9 @@
         pltpu.make_async_copy(whole, whole, sem_b).wait()
 
 
-def rotate_kernel(recv, rows, out, recv_v, rows_v, out_v, sems):
-    load = pltpu.make_async_copy(recv, recv_v, sems.at[0])
-    load_rows = pltpu.make_async_copy(rows, rows_v, sems.at[1])
-    load.start()
-    load_rows.start()
-    load_rows.wait()
+def rotate_kernel(recv_v, rows_v, out, out_v, sems):
     high, low = two_parts(jnp.concatenate([rows_v[:, 0], rows_v[:, 1]], axis=0).T)
     matrix = jnp.concatenate([high, high, low], axis=1)
-    load.wait()
     width = 256
     stores = []
     for at in range(0, 8 * 128, width):
@@ -297,7 +285,7 @@
             matrix, jnp.concatenate(columns, axis=1), preferred_element_type=jnp.float32
         )
         store = pltpu.make_async_copy(
-            out_v.at[:, pl.ds(at, width)], out.at[:, pl.ds(at, width)], sems.at[2 + at // width]
+            out_v.at[:, pl.ds(at, width)], out.at[:, pl.ds(at, width)], sems.at[at // width]
         )
         store.start()
         stores.append(store)
@@ -315,16 +303,17 @@
     recv, rows = pl.pallas_call(
         functools.partial(filter_kernel, bands, doms),
         out_shape=(
-            jax.ShapeDtypeStruct((bands, orbs, 8, 128), f32),
-            jax.ShapeDtypeStruct((bands, orbs, 128), f32),
+            pltpu.VMEM((bands, orbs, 8, 128), f32),
+            pltpu.VMEM((bands, orbs, 128), f32),
         ),
         in_specs=[anywhere] * 3,
         out_specs=(anywhere,) * 2,
         scratch_shapes=[
             *[
                 pltpu.VMEM((orbs, planes + 2 * REACH * (DEG - level), 2, 8, 128), f32)
-                for level in range(DEG + 1)
+                for level in range(DEG)
             ],
+            pltpu.VMEM((orbs, bands, 8, 128), f32),
             pltpu.VMEM((planes + 2 * REACH * (DEG - 1), 2, 8, 128), f32),
             dma((orbs,)),
             dma((orbs,)),
@@ -339,24 +328,19 @@
             dma,
         ],
         compiler_params=pltpu.CompilerParams(
-            collective_id=0, has_side_effects=True, vmem_limit_bytes=60 * 2**20
+            collective_id=0, has_side_effects=True, vmem_limit_bytes=32 * 2**20
         ),
         name="filter",
-    )(orb, pot, subspace)
+    )(*(pltpu.with_memory_space_constraint(a, pltpu.HBM) for a in (orb, pot, subspace)))
     return pl.pallas_call(
         rotate_kernel,
         out_shape=jax.ShapeDtypeStruct((bands * orbs, 1024), f32),
-        in_specs=[anywhere] * 2,
+        in_specs=[pl.BlockSpec(memory_space=pltpu.VMEM)] * 2,
         out_specs=anywhere,
-        scratch_shapes=[
-            pltpu.VMEM((bands, orbs, 8, 128), f32),
-            pltpu.VMEM((bands, orbs, 128), f32),
-            pltpu.VMEM((bands * orbs, 1024), f32),
-            dma((6,)),
-        ],
-        compiler_params=pltpu.CompilerParams(vmem_limit_bytes=60 * 2**20),
+        scratch_shapes=[pltpu.VMEM((bands * orbs, 1024), f32), dma((4,))],
+        compiler_params=pltpu.CompilerParams(vmem_limit_bytes=32 * 2**20),
         name="rotate",
-    )(recv, rows)
+    )(*(pltpu.with_memory_space_constraint(a, pltpu.VMEM) for a in (recv, rows)))
 
 
 def solution(mesh):

time: 44.8 us -> 43.5 us (0.971)
  Pallas kernels: 44.7 us -> 43.4 us
    pallas_call x1, Pallas kernels: 2.4 us -> 1.31 us  [per_device(): pl.pallas_call(rotate_kernel, out_shape=jax.ShapeDtypeStruct((bands * orb...]
where the time goes in v1:
time: 43.5 us; the launch traced here: 43.4 us
  Pallas kernels  43.4 us (100%)
    pallas_call x1, Pallas kernels, per_device(): pl.pallas_call(functools.partial(filter_kernel, bands, doms), out_shape=(...  42.1 us
    pallas_call x1, Pallas kernels, per_device(): pl.pallas_call(rotate_kernel, out_shape=jax.ShapeDtypeStruct((bands * orb...  1.31 us

profile of v1, /device:TPU:1, one launch (start us, length us, event | category | flops | bytes accessed | tf_op | source)
XLA Modules:
  0.0 43.4 jit_solution(14296566578590490360)
XLA Ops:
  0.0 42.1 %filter.1 = (f32[64,2,8,128]{3,2,1,0:T(8,128)S(1)}, f32[64,2,128]{2,1,0:T(2,128)S(1)}) custom-call(f32[2,32,2,8,128]{4,3,2,1,0:T(8,128)} %bitcast.2, f32[32,2,8,128]{3,2,1,0:T(8,128)} %bitcast.3, f32[2,128]{1,0:T(2,128)} %sub.1), custom_call_target="tpu_custom_call" | custom-call | tf_op jit(solution)/shard_map/filter/pallas_call | solution.py:303
  42.1 1.3 %rotate.1 = f32[128,1024]{1,0:T(8,128)} custom-call(f32[64,2,8,128]{3,2,1,0:T(8,128)S(1)} %get-tuple-element.7.recv_v, f32[64,2,128]{2,1,0:T(2,128)S(1)} %get-tuple-element.8.rows_v), custom_call_target="tpu_custom_call" | custom-call | tf_op jit(solution)/shard_map/rotate/pallas_call | solution.py:335

commit v2 on v1

--- a/solution.py
+++ b/solution.py
@@ -188,11 +188,27 @@
         nears.append(near)
         fars.append(far)
 
-    own_rows = pltpu.make_async_copy(sub, rows.at[band], move_sem.at[2])
+    own_rows = pltpu.make_async_copy(sub, rows.at[zl, y, x], move_sem.at[2])
     own_rows.start()
-
-    for peer in others:
-        remote(sub, rows.at[band], row_send, row_recv, {"band": peer}).start()
+    lines = [
+        (rows.at[zl, y, x], [along_z[d] + along_y[0] + along_x[0] for d in range(1, side)]),
+        (rows.at[:, y, x], [along_z[0] + along_y[d] + along_x[0] for d in range(1, side)]),
+        (rows.at[:, :, x], [along_z[0] + along_y[0] + along_x[d] for d in range(1, side)]),
+    ]
+
+    def send_rows(stage):
+        mine, peers = lines[stage]
+        copies = [
+            remote(mine, mine, row_send.at[stage, at], row_recv.at[stage, at], {"band": peer})
+            for at, peer in enumerate(peers)
+        ]
+        for copy in copies:
+            copy.start()
+        return copies
+
+    own_rows.wait()
+    row_copies = [send_rows(0)]
+
 
     def apply(level, o, begin, blocks):
         scale, weight = scalars[level]
@@ -212,7 +228,7 @@
                 buffers[level + 1][o, pl.ds(at + rims[level + 1], step), 1] = high
             else:
                 pairs = jnp.stack([low, high], axis=1)
-                out[o, pl.ds(2 * at, 2 * step)] = pairs.reshape(2 * step, 8, 128)
+                out[pl.ds(2 * at, 2 * step), o] = pairs.reshape(2 * step, 8, 128)
             return c
 
         lax.fori_loop(0, blocks, body, 0)
@@ -227,6 +243,9 @@
             rim = rims[level + 1]
             apply(level, o, core * -rim + (1 - core) * (20 - rim), early[level])
 
+    for copy in row_copies[0]:
+        copy.wait_recv()
+    row_copies.append(send_rows(1))
     pot_far.wait_recv()
     at_far = (planes + pot_rim) * core + x * part
     passed = []
@@ -236,38 +255,34 @@
         copy = remote(mine, mine, pot_send.at[1 + d], pot_recv.at[1 + d], peer)
         copy.start()
         passed.append(copy)
+    for copy in row_copies[1]:
+        copy.wait_recv()
+    row_copies.append(send_rows(2))
     for copy in passed:
         copy.wait_recv()
 
-    def spread(o):
-        own = pltpu.make_async_copy(
-            out.at[o, band], recv.at[band, o], move_sem.at[3 + o]
-        )
-        own.start()
-
-        for peer in others:
-            remote(
-                out.at[o, peer], recv.at[band, o], all_send, all_recv, {"band": peer}
-            ).start()
-        return own
-
-    owns = []
     for o in range(orbs):
         fars[o].wait_recv()
         for level in range(DEG):
             rim = rims[level + 1]
             apply(level, o, core * (planes + rim - 20) - (1 - core) * rim, 20 // step)
-        owns.append(spread(o))
+
+    for peer in others:
+        remote(out.at[peer], recv.at[band], all_send, all_recv, {"band": peer}).start()
+    own = pltpu.make_async_copy(out.at[band], recv.at[band], move_sem.at[3])
+    own.start()
 
     for copy in (*nears, *fars, pot_far, pot_near, *passed):
         copy.wait_send()
-    own_rows.wait()
-    for own in owns:
-        own.wait()
-    for ref, sem_a, sem_b in ((rows, row_send, row_recv), (recv, all_send, all_recv)):
-        whole = ref.at[pl.ds(0, bands - 1)]
-        pltpu.make_async_copy(whole, whole, sem_a).wait()
-        pltpu.make_async_copy(whole, whole, sem_b).wait()
+    for stage in row_copies:
+        for copy in stage:
+            copy.wait_send()
+    for copy in row_copies[2]:
+        copy.wait_recv()
+    own.wait()
+    whole = recv.at[pl.ds(0, bands - 1)]
+    pltpu.make_async_copy(whole, whole, all_send).wait()
+    pltpu.make_async_copy(whole, whole, all_recv).wait()
 
 
 def rotate_kernel(recv_v, rows_v, out, out_v, sems):
@@ -304,7 +319,7 @@
         functools.partial(filter_kernel, bands, doms),
         out_shape=(
             pltpu.VMEM((bands, orbs, 8, 128), f32),
-            pltpu.VMEM((bands, orbs, 128), f32),
+            pltpu.VMEM((4, 4, 4, orbs, 128), f32),
         ),
         in_specs=[anywhere] * 3,
         out_specs=(anywhere,) * 2,
@@ -313,7 +328,7 @@
                 pltpu.VMEM((orbs, planes + 2 * REACH * (DEG - level), 2, 8, 128), f32)
                 for level in range(DEG)
             ],
-            pltpu.VMEM((orbs, bands, 8, 128), f32),
+            pltpu.VMEM((bands, orbs, 8, 128), f32),
             pltpu.VMEM((planes + 2 * REACH * (DEG - 1), 2, 8, 128), f32),
             dma((orbs,)),
             dma((orbs,)),
@@ -321,11 +336,11 @@
             dma((orbs,)),
             dma((5,)),
             dma((5,)),
-            dma((3 + orbs,)),
+            dma((4,)),
             dma,
             dma,
-            dma,
-            dma,
+            dma((3, 3)),
+            dma((3, 3)),
         ],
         compiler_params=pltpu.CompilerParams(
             collective_id=0, has_side_effects=True, vmem_limit_bytes=32 * 2**20
@@ -340,7 +355,7 @@
         scratch_shapes=[pltpu.VMEM((bands * orbs, 1024), f32), dma((4,))],
         compiler_params=pltpu.CompilerParams(vmem_limit_bytes=32 * 2**20),
         name="rotate",
-    )(*(pltpu.with_memory_space_constraint(a, pltpu.VMEM) for a in (recv, rows)))
+    )(*(pltpu.with_memory_space_constraint(a, pltpu.VMEM) for a in (recv, rows.reshape(bands, orbs, 128))))
 
 
 def solution(mesh):

time: 43.5 us -> 50 us (1.15)
  the two profiles are of different devices: /device:TPU:1 before, /device:TPU:6 now
where the time goes in v2:
time: 50 us; the launch traced here: 49.9 us
  Pallas kernels  49.9 us (100%)
    pallas_call x1, Pallas kernels, per_device(): pl.pallas_call(functools.partial(filter_kernel, bands, doms), out_shape=(...  48.6 us
    pallas_call x1, Pallas kernels, per_device(): pl.pallas_call(rotate_kernel, out_shape=jax.ShapeDtypeStruct((bands * orb...  1.31 us

profile of v2, /device:TPU:6, one launch (start us, length us, event | category | flops | bytes accessed | tf_op | source)
XLA Modules:
  0.0 49.9 jit_solution(11164315244102962796)
XLA Ops:
  0.0 48.6 %filter.1 = (f32[64,2,8,128]{3,2,1,0:T(8,128)S(1)}, f32[4,4,4,2,128]{4,3,2,1,0:T(2,128)S(1)}) custom-call(f32[2,32,2,8,128]{4,3,2,1,0:T(8,128)} %bitcast.4, f32[32,2,8,128]{3,2,1,0:T(8,128)} %bitcast.5, f32[2,128]{1,0:T(2,128)} %sub.1), custom_call_target="tpu_custom_call" | custom-call | tf_op jit(solution)/shard_map/filter/pallas_call | solution.py:318
  48.6 1.3 %rotate.1 = f32[128,1024]{1,0:T(8,128)} custom-call(f32[64,2,8,128]{3,2,1,0:T(8,128)S(1)} %get-tuple-element.7.recv_v, f32[64,2,128]{2,1,0:T(2,128)S(1)} %bitcast.3), custom_call_target="tpu_custom_call" | custom-call | tf_op jit(solution)/shard_map/rotate/pallas_call | solution.py:350

commit v3 on v1

v3 whole, which is shorter than its diff:
```python
import functools
import math

import jax
import jax.numpy as jnp
from jax import lax
from jax.experimental import pallas as pl
from jax.experimental.pallas import tpu as pltpu
from jax.sharding import PartitionSpec as P

DEG = 3
REACH = 6
MESH = pl.DeviceIdType.MESH

upper_edge = 10.7
lower_edge = 1.5
bottom_edge = -1.0


def stencil_weights():
    factor_square = math.factorial(6) ** 2
    side_weights = []
    for offset in range(1, 7):
        side_weights.append(
            2.0
            * (-1.0) ** (offset + 1)
            * factor_square
            / (offset * offset * math.factorial(6 - offset) * math.factorial(6 + offset))
        )
    center_weight = -2.0 * sum(side_weights)
    return (center_weight, side_weights)


def filter_scalars(pass_count):
    half_width = (upper_edge - lower_edge) / 2.0
    sigma_now = half_width / (bottom_edge - (upper_edge + lower_edge) / 2.0)
    gamma_value = 2.0 / sigma_now
    scalars = [(sigma_now / half_width, 0.0)]
    for pass_index in range(pass_count - 1):
        sigma_next = 1.0 / (gamma_value - sigma_now)
        scalars.append((2.0 * sigma_next / half_width, sigma_now * sigma_next))
        sigma_now = sigma_next
    return scalars


def two_parts(values):
    high = values.astype(jnp.bfloat16)
    return high, (values - high.astype(jnp.float32)).astype(jnp.bfloat16)


def lane_matrix():
    rows = lax.broadcasted_iota(jnp.int32, (128, 128), 0)
    columns = lax.broadcasted_iota(jnp.int32, (128, 128), 1)
    apart = jnp.abs(rows - columns)
    apart = jnp.minimum(apart, 128 - apart)
    matrix = jnp.zeros((128, 128), jnp.float32)
    for k, w in enumerate(stencil_weights()[1], 1):
        matrix = jnp.where(apart == k, jnp.float32(w), matrix)
    high, low = two_parts(matrix)
    return jnp.concatenate([high, high, low], axis=0)


def row_weights():
    side = stencil_weights()[1]
    weight = lambda k: side[k - 1] if 1 <= k <= REACH else 0.0
    rows = lax.broadcasted_iota(jnp.int32, (8, 128), 0)
    cyclic, negacyclic = {}, {}
    for r in range(1, 8):
        cyclic[r] = 0.5 * (weight(r) + weight(8 - r))
        if r != 4:
            w = 0.5 * (weight(r) - weight(8 - r))
            negacyclic[r] = jnp.where(rows >= r, jnp.float32(w), jnp.float32(-w))
    return cyclic, negacyclic


def filtered_block(window, pot, before, scale, weight, lanes, cyclic, negacyclic):
    center_weight, side = stencil_weights()
    n = window.shape[0] - 2 * REACH
    mid = window[REACH : REACH + n]
    high, low = two_parts(mid.reshape(n * 16, 128))
    total = jnp.dot(
        jnp.concatenate([high, low, high], axis=1), lanes, preferred_element_type=jnp.float32
    ).reshape(n, 2, 8, 128)
    for k in range(1, REACH + 1):
        beside = window[REACH + k : REACH + k + n] + window[REACH - k : REACH - k + n]
        total = total + side[k - 1] * beside
    both, apart = mid[:, 0] + mid[:, 1], mid[:, 0] - mid[:, 1]
    even = cyclic[4] * pltpu.roll(both, 4, 1)
    for r in range(1, 4):
        even = even + cyclic[r] * (pltpu.roll(both, r, 1) + pltpu.roll(both, 8 - r, 1))
    odd = None
    for r, w in negacyclic.items():
        term = w * pltpu.roll(apart, r, 1)
        odd = term if odd is None else odd + term
    diag = (-1.5 * center_weight - (upper_edge + lower_edge) / 2.0) * scale
    results = []
    for at, rows in enumerate((even + odd, even - odd)):
        result = (pot[:, at] * scale + diag) * mid[:, at]
        result = result + (-0.5 * scale) * (total[:, at] + rows)
        if before is not None:
            result = result - weight * before[:, at]
        results.append(result)
    return results


def filter_kernel(
    bands, orb, pot, sub, recv, rows, p0, p1, p2, out, pot_v,
    near_send, near_recv, far_send, far_recv, pot_send, pot_recv, pass_send, pass_recv,
    move_sem, all_send, all_recv, row_send, row_recv,
):
    quarter = orb.shape[1]
    slab, whole = 2 * quarter, 4 * quarter
    band, dom = lax.axis_index("band"), lax.axis_index("dom")
    core, half = lax.rem(dom, 2), lax.div(dom, 2)
    side = 4
    floor = side * side
    zl, x, yx = lax.div(band, floor), lax.rem(band, side), lax.rem(band, floor)
    shift = 2 * REACH
    left = jnp.where(zl < side // 2, 1, 0)
    long = core == left
    base = half * slab
    own_tile = dom * bands + band
    own_plane = lax.div(own_tile, 2)
    scalars = filter_scalars(DEG)
    buffers = (p0, p1, p2)
    rims = tuple(shift + REACH * (DEG - level) for level in range(DEG + 1))
    pot_rim = rims[1]
    step = 4

    def placed(u, count):
        return jnp.where(left == 1, u, slab - count - u)

    load = pltpu.make_async_copy(
        orb.at[core], p0.at[pl.ds(core * quarter + rims[0], quarter)], move_sem.at[0]
    )
    load.start()
    load_pot = pltpu.make_async_copy(
        pot, pot_v.at[pl.ds(core * quarter + pot_rim, quarter)], move_sem.at[1]
    )
    load_pot.start()

    sibling = {"dom": dom + 1 - 2 * core}
    partners = [{"dom": 2 * (1 - half) + k} for k in range(2)]

    barrier = pltpu.get_barrier_semaphore()
    for peer in partners:
        pl.semaphore_signal(barrier, inc=1, device_id=peer, device_id_type=MESH)
    in_left = (own_plane >= slab - shift) & (own_plane < whole - shift)
    in_right = (own_plane >= slab + shift) | (own_plane < shift)
    for line in range(side):
        there = jnp.where(in_left if line < side // 2 else in_right, 2, 0)
        for k in range(2):

            def greet(i, c, line=line, k=k, there=there):
                peer = line * floor + lax.rem(yx + i, floor)

                @pl.when((peer != band) | (there + k != dom))
                def _():
                    pl.semaphore_signal(
                        barrier, inc=1, device_id={"band": peer, "dom": there + k},
                        device_id_type=MESH,
                    )

                return c

            lax.fori_loop(0, floor, greet, 0)
    lanes = lane_matrix()
    cyclic, negacyclic = row_weights()
    pl.semaphore_wait(barrier, 2 * bands + 1)

    def remote(src, dst, send_sem, recv_sem, peer):
        return pltpu.make_async_remote_copy(
            src_ref=src, dst_ref=dst, send_sem=send_sem, recv_sem=recv_sem,
            device_id=peer, device_id_type=MESH,
        )

    pieces = [(0, REACH)] + [(REACH + 8 * i, 8) for i in range(3)]
    assert sum(n for _, n in pieces) == rims[0]
    far = []
    for o in range(2):
        group = []
        for at, (a, n) in enumerate(pieces):
            group.append(
                remote(
                    orb.at[o, pl.ds(jnp.where(left == 1, quarter - a - n, a), n)],
                    p0.at[pl.ds(placed(-a - n, n) + rims[0], n)],
                    far_send.at[o, at], far_recv.at[at], partners[o],
                )
            )
        n = REACH
        group.append(
            remote(
                orb.at[o, pl.ds(jnp.where(left == 1, 0, quarter - n), n)],
                p0.at[pl.ds(placed(slab, n) + rims[0], n)],
                far_send.at[o, 4], far_recv.at[4], partners[o],
            )
        )
        far.append(group)
    part = pot_rim // 8
    pot_far = [
        remote(
            pot.at[pl.ds(jnp.where(left == 1, quarter - pot_rim, 0) + (2 * x + o) * part, part)],
            pot_v.at[pl.ds(placed(-pot_rim, pot_rim) + pot_rim + (2 * x + o) * part, part)],
            pot_send.at[o], pot_recv, partners[o],
        )
        for o in range(2)
    ]
    mine = pot_v.at[pl.ds(placed(-pot_rim, pot_rim) + pot_rim + (2 * x + core) * part, part)]

    @pl.when(long)
    def _():
        for o in range(2):
            pot_far[o].start()
        for o in range(2):
            far[o][0].start()

    @pl.when(jnp.logical_not(long))
    def _():
        for o in range(2):
            far[o][4].start()

    near = remote(
        orb.at[1 - core], p0.at[pl.ds(core * quarter + rims[0], quarter)],
        near_send.at[0], near_recv.at[0], sibling,
    )
    near_pot = remote(
        pot, pot_v.at[pl.ds(core * quarter + pot_rim, quarter)],
        near_send.at[1], near_recv.at[1], sibling,
    )
    near.start()
    near_pot.start()

    @pl.when(long)
    def _():
        for at in range(1, 4):
            for o in range(2):
                far[o][at].start()

    def send_rows(i, c):
        at = lax.rem(i + band, bands)
        plane = core * quarter + lax.div(at, 2)
        plane = jnp.where(
            left == 1,
            jnp.where(plane >= slab - shift, plane - slab, plane),
            jnp.where(plane < shift, plane + slab, plane),
        )
        tile = lax.rem(2 * (base + plane) + lax.rem(at, 2) + 2 * whole, 2 * whole)

        @pl.when(tile != own_tile)
        def _():
            peer = {"band": lax.rem(tile, bands), "dom": lax.div(tile, bands)}
            remote(sub, rows.at[band], row_send, row_recv, peer).start()

        return c

    lax.fori_loop(0, bands, send_rows, 0)
    own_rows = pltpu.make_async_copy(sub, rows.at[band], move_sem.at[2])
    own_rows.start()

    def apply(level, u, blocks):
        scale, weight = scalars[level]

        def body(i, c):
            at = placed(u + i * step, step)
            before = None
            if level > 0:
                before = buffers[level - 1][pl.ds(at + rims[level - 1], step)]
            window = buffers[level][pl.ds(at + rims[level] - REACH, step + 2 * REACH)]
            low, high = filtered_block(
                window, pot_v[pl.ds(at + pot_rim, step)], before, scale, weight,
                lanes, cyclic, negacyclic,
            )
            pairs = jnp.stack([low, high], axis=1)
            if level < DEG - 1:
                buffers[level + 1][pl.ds(at + rims[level + 1], step)] = pairs
            else:
                out[pl.ds(2 * (at + rims[DEG]), 2 * step)] = pairs.reshape(2 * step, 8, 128)
            return c

        lax.fori_loop(0, blocks, body, 0)

    row = 2 * band + core

    def spread(u, count):
        start = placed(u, count)
        tiles = 2 * count

        def send(i, c):
            at = lax.rem(i + yx * (tiles // floor), tiles)
            tile = lax.rem(2 * (base + start) + at + 2 * whole, 2 * whole)
            src = out.at[2 * (start + rims[DEG]) + at]

            @pl.when(tile != own_tile)
            def _():
                peer = {"band": lax.rem(tile, bands), "dom": lax.div(tile, bands)}
                remote(src, recv.at[row], all_send, all_recv, peer).start()

            @pl.when(tile == own_tile)
            def _():
                pltpu.make_async_copy(src, recv.at[row], move_sem.at[3]).start()

            return c

        lax.fori_loop(0, tiles, send, 0)

    def advance(u, blocks):
        for level in range(DEG):
            apply(level, u + level * REACH, blocks)
        spread(u + (DEG - 1) * REACH, blocks * step)

    load.wait()
    load_pot.wait()
    near.wait_recv()
    near_pot.wait_recv()
    apply(0, 8, 12)
    apply(1, 14, 9)
    apply(2, 20, 6)
    spread(20, 24)

    pot_far[0].wait_recv()
    passed = []
    for dx in range(side):
        for dk in range(2):
            if dx or dk:
                peer = {
                    "band": band - x + lax.rem(x + dx, side),
                    "dom": dom if dk == 0 else dom + 1 - 2 * core,
                }
                at = 2 * dx + dk - 1
                passed.append(remote(mine, mine, pass_send.at[at], pass_recv.at[at], peer))
    for copy in passed:
        copy.start()

    far[0][4].wait_recv()
    apply(0, slab - 8, 2)
    apply(1, slab - 14, 2)
    apply(2, slab - 20, 2)
    spread(slab - 20, 8)
    for at in range(4):
        if at == 1:
            for copy in passed:
                copy.wait_recv()
        far[0][at].wait_recv()
        advance(-8 * at, 2)

    @pl.when(long)
    def _():
        for o in range(2):
            pot_far[o].wait_send()
            for at in range(4):
                far[o][at].wait_send()

    @pl.when(jnp.logical_not(long))
    def _():
        for o in range(2):
            far[o][4].wait_send()

    for copy in (near, near_pot, *passed):
        copy.wait_send()
    own_rows.wait()
    pltpu.make_async_copy(out.at[0], recv.at[row], move_sem.at[3]).wait()
    for ref, sem_a, sem_b in ((rows, row_send, row_recv), (recv, all_send, all_recv)):
        all_but_own = ref.at[pl.ds(0, ref.shape[0] - 1)]
        pltpu.make_async_copy(all_but_own, all_but_own, sem_a).wait()
        pltpu.make_async_copy(all_but_own, all_but_own, sem_b).wait()


def rotate_kernel(recv_v, rows_v, out, out_v, sems):
    high, low = two_parts(jnp.concatenate([rows_v[:, 0], rows_v[:, 1]], axis=0).T)
    matrix = jnp.concatenate([high, high, low], axis=1)
    width = 256
    stores = []
    for at in range(0, 8 * 128, width):
        columns = []
        for r in range(at // 128, (at + width) // 128):
            values = jnp.concatenate([recv_v[:, 0, r], recv_v[:, 1, r]], axis=0)
            high, low = two_parts(values)
            columns.append(jnp.concatenate([high, low, high], axis=0))
        out_v[:, pl.ds(at, width)] = jnp.dot(
            matrix, jnp.concatenate(columns, axis=1), preferred_element_type=jnp.float32
        )
        store = pltpu.make_async_copy(
            out_v.at[:, pl.ds(at, width)], out.at[:, pl.ds(at, width)], sems.at[at // width]
        )
        store.start()
        stores.append(store)
    for store in stores:
        store.wait()


def per_device(bands, orbitals, potential, subspace):
    orbs, planes = orbitals.shape[0], orbitals.shape[1]
    orb = orbitals.reshape(orbs, planes, 2, 8, 128)
    pot = potential.reshape(planes, 2, 8, 128)
    f32 = jnp.float32
    dma = pltpu.SemaphoreType.DMA
    anywhere = pl.BlockSpec(memory_space=pl.ANY)
    slab, shift = 2 * planes, 2 * REACH
    recv, rows = pl.pallas_call(
        functools.partial(filter_kernel, bands),
        out_shape=(
            pltpu.VMEM((bands * orbs, 8, 128), f32),
            pltpu.VMEM((bands, orbs, 128), f32),
        ),
        in_specs=[anywhere] * 3,
        out_specs=(anywhere,) * 2,
        scratch_shapes=[
            *[
                pltpu.VMEM((slab + 2 * (shift + REACH * (DEG - level)), 2, 8, 128), f32)
                for level in range(DEG)
            ],
            pltpu.VMEM((2 * (slab + 2 * shift), 8, 128), f32),
            pltpu.VMEM((slab + 2 * (shift + REACH * (DEG - 1)), 2, 8, 128), f32),
            dma((2,)),
            dma((2,)),
            dma((2, 5)),
            dma((5,)),
            dma((2,)),
            dma,
            dma((7,)),
            dma((7,)),
            dma((4,)),
            dma,
            dma,
            dma,
            dma,
        ],
        compiler_params=pltpu.CompilerParams(
            collective_id=0, has_side_effects=True, vmem_limit_bytes=32 * 2**20
        ),
        name="filter",
    )(*(pltpu.with_memory_space_constraint(a, pltpu.HBM) for a in (orb, pot, subspace)))
    recv = recv.reshape(bands, orbs, 8, 128)
    return pl.pallas_call(
        rotate_kernel,
        out_shape=jax.ShapeDtypeStruct((bands * orbs, 1024), f32),
        in_specs=[pl.BlockSpec(memory_space=pltpu.VMEM)] * 2,
        out_specs=anywhere,
        scratch_shapes=[pltpu.VMEM((bands * orbs, 1024), f32), dma((4,))],
        compiler_params=pltpu.CompilerParams(vmem_limit_bytes=32 * 2**20),
        name="rotate",
    )(*(pltpu.with_memory_space_constraint(a, pltpu.VMEM) for a in (recv, rows)))


def solution(mesh):
    in_specs = (P("band", "dom", None, None), P("dom", None, None), P("band", None))
    out_specs = P(None, ("dom", "band"))
    return jax.shard_map(
        functools.partial(per_device, mesh.shape["band"]),
        mesh=mesh,
        in_specs=in_specs,
        out_specs=out_specs,
        check_vma=False,
    )
```

time: 43.5 us -> 42.9 us (0.986)
  the two profiles are of different devices: /device:TPU:1 before, /device:TPU:32 now
where the time goes in v3:
time: 42.9 us; the launch traced here: 42.4 us
  Pallas kernels  42.4 us (99%)
    pallas_call x1, Pallas kernels, per_device(): pl.pallas_call(functools.partial(filter_kernel, bands), out_shape=(pltpu....  41.1 us
    pallas_call x1, Pallas kernels, per_device(): pl.pallas_call(rotate_kernel, out_shape=jax.ShapeDtypeStruct((bands * orb...  1.31 us

profile of v3, /device:TPU:32, one launch (start us, length us, event | category | flops | bytes accessed | tf_op | source)
XLA Modules:
  0.0 42.4 jit_solution(14069261291544236131)
XLA Ops:
  0.0 41.1 %filter.1 = (f32[128,8,128]{2,1,0:T(8,128)S(1)}, f32[64,2,128]{2,1,0:T(2,128)S(1)}) custom-call(f32[2,32,2,8,128]{4,3,2,1,0:T(8,128)} %bitcast.4, f32[32,2,8,128]{3,2,1,0:T(8,128)} %bitcast.5, f32[2,128]{1,0:T(2,128)} %sub.1), custom_call_target="tpu_custom_call" | custom-call | tf_op jit(solution)/shard_map/filter/pallas_call | solution.py:399
  41.1 1.3 %rotate.1 = f32[128,1024]{1,0:T(8,128)} custom-call(f32[64,2,8,128]{3,2,1,0:T(8,128)S(1)} %bitcast.3, f32[64,2,128]{2,1,0:T(2,128)S(1)} %get-tuple-element.8.rows_v), custom_call_target="tpu_custom_call" | custom-call | tf_op jit(solution)/shard_map/rotate/pallas_call | solution.py:434

commit v4 on v3

--- a/solution.py
+++ b/solution.py
@@ -125,7 +125,6 @@
     buffers = (p0, p1, p2)
     rims = tuple(shift + REACH * (DEG - level) for level in range(DEG + 1))
     pot_rim = rims[1]
-    step = 4
 
     def placed(u, count):
         return jnp.where(left == 1, u, slab - count - u)
@@ -257,7 +256,7 @@
     own_rows = pltpu.make_async_copy(sub, rows.at[band], move_sem.at[2])
     own_rows.start()
 
-    def apply(level, u, blocks):
+    def apply(level, u, blocks, step):
         scale, weight = scalars[level]
 
         def body(i, c):
@@ -303,18 +302,18 @@
 
         lax.fori_loop(0, tiles, send, 0)
 
-    def advance(u, blocks):
+    def advance(u):
         for level in range(DEG):
-            apply(level, u + level * REACH, blocks)
-        spread(u + (DEG - 1) * REACH, blocks * step)
+            apply(level, u + level * REACH, 1, 8)
+        spread(u + (DEG - 1) * REACH, 8)
 
     load.wait()
     load_pot.wait()
     near.wait_recv()
     near_pot.wait_recv()
-    apply(0, 8, 12)
-    apply(1, 14, 9)
-    apply(2, 20, 6)
+    apply(0, 8, 4, 12)
+    apply(1, 14, 3, 12)
+    apply(2, 20, 2, 12)
     spread(20, 24)
 
     pot_far[0].wait_recv()
@@ -332,16 +331,16 @@
         copy.start()
 
     far[0][4].wait_recv()
-    apply(0, slab - 8, 2)
-    apply(1, slab - 14, 2)
-    apply(2, slab - 20, 2)
+    apply(0, slab - 8, 1, 8)
+    apply(1, slab - 14, 1, 8)
+    apply(2, slab - 20, 1, 8)
     spread(slab - 20, 8)
     for at in range(4):
         if at == 1:
             for copy in passed:
                 copy.wait_recv()
         far[0][at].wait_recv()
-        advance(-8 * at, 2)
+        advance(-8 * at)
 
     @pl.when(long)
     def _():

time: 42.9 us -> 42.4 us (0.988)
  no operation moved by 1% of the time
where the time goes in v4:
time: 42.4 us; the launch traced here: 42 us
  Pallas kernels  42 us (99%)
    pallas_call x1, Pallas kernels, per_device(): pl.pallas_call(functools.partial(filter_kernel, bands), out_shape=(pltpu....  40.7 us
    pallas_call x1, Pallas kernels, per_device(): pl.pallas_call(rotate_kernel, out_shape=jax.ShapeDtypeStruct((bands * orb...  1.31 us

profile of v4, /device:TPU:32, one launch (start us, length us, event | category | flops | bytes accessed | tf_op | source)
XLA Modules:
  0.0 42.0 jit_solution(9792338995480030453)
XLA Ops:
  0.0 40.7 %filter.1 = (f32[128,8,128]{2,1,0:T(8,128)S(1)}, f32[64,2,128]{2,1,0:T(2,128)S(1)}) custom-call(f32[2,32,2,8,128]{4,3,2,1,0:T(8,128)} %bitcast.4, f32[32,2,8,128]{3,2,1,0:T(8,128)} %bitcast.5, f32[2,128]{1,0:T(2,128)} %sub.1), custom_call_target="tpu_custom_call" | custom-call | tf_op jit(solution)/shard_map/filter/pallas_call | solution.py:398
  40.7 1.3 %rotate.1 = f32[128,1024]{1,0:T(8,128)} custom-call(f32[64,2,8,128]{3,2,1,0:T(8,128)S(1)} %bitcast.3, f32[64,2,128]{2,1,0:T(2,128)S(1)} %get-tuple-element.8.rows_v), custom_call_target="tpu_custom_call" | custom-call | tf_op jit(solution)/shard_map/rotate/pallas_call | solution.py:433

commit v5 on v4

--- a/solution.py
+++ b/solution.py
@@ -104,8 +104,8 @@
 
 
 def filter_kernel(
-    bands, orb, pot, sub, recv, rows, p0, p1, p2, out, pot_v,
-    near_send, near_recv, far_send, far_recv, pot_send, pot_recv, pass_send, pass_recv,
+    bands, orb, pot, sub, recv, rows, p0, p1, p2, out, pot_v, held,
+    near_send, near_recv, far_send, far_recv, onward_send, onward_recv, pot_send, pot_recv, pass_send, pass_recv,
     move_sem, all_send, all_recv, row_send, row_recv,
 ):
     quarter = orb.shape[1]
@@ -141,8 +141,19 @@
     sibling = {"dom": dom + 1 - 2 * core}
     partners = [{"dom": 2 * (1 - half) + k} for k in range(2)]
 
+    def chip_along(shift, core_there):
+        there = lax.rem(half * side + zl + shift + 2 * side, 2 * side)
+        return {
+            "band": lax.rem(there, side) * floor + yx,
+            "dom": lax.div(there, side) * 2 + core_there,
+        }
+
+    relays = [chip_along(2 - 4 * o, o) for o in range(2)]
+    onward_to = chip_along(2 - 4 * core, core)
+    relay_from = [chip_along(4 * core - 2, k) for k in range(2)]
+
     barrier = pltpu.get_barrier_semaphore()
-    for peer in partners:
+    for peer in (*partners, *relay_from):
         pl.semaphore_signal(barrier, inc=1, device_id=peer, device_id_type=MESH)
     in_left = (own_plane >= slab - shift) & (own_plane < whole - shift)
     in_right = (own_plane >= slab + shift) | (own_plane < shift)
@@ -165,7 +176,7 @@
             lax.fori_loop(0, floor, greet, 0)
     lanes = lane_matrix()
     cyclic, negacyclic = row_weights()
-    pl.semaphore_wait(barrier, 2 * bands + 1)
+    pl.semaphore_wait(barrier, 2 * bands + 3)
 
     def remote(src, dst, send_sem, recv_sem, peer):
         return pltpu.make_async_remote_copy(
@@ -175,26 +186,41 @@
 
     pieces = [(0, REACH)] + [(REACH + 8 * i, 8) for i in range(3)]
     assert sum(n for _, n in pieces) == rims[0]
-    far = []
-    for o in range(2):
-        group = []
-        for at, (a, n) in enumerate(pieces):
-            group.append(
-                remote(
-                    orb.at[o, pl.ds(jnp.where(left == 1, quarter - a - n, a), n)],
-                    p0.at[pl.ds(placed(-a - n, n) + rims[0], n)],
-                    far_send.at[o, at], far_recv.at[at], partners[o],
-                )
+    pieces.append((slab, REACH))
+    far = [
+        [
+            remote(
+                orb.at[
+                    o,
+                    pl.ds(
+                        jnp.where(left == 1, 0, quarter - n)
+                        if a == slab
+                        else jnp.where(left == 1, quarter - a - n, a),
+                        n,
+                    ),
+                ],
+                held.at[at, pl.ds(0, n)], far_send.at[o, at], far_recv.at[at], relays[o],
             )
-        n = REACH
-        group.append(
+            for at, (a, n) in enumerate(pieces)
+        ]
+        for o in range(2)
+    ]
+    onward = []
+    for at, (a, n) in enumerate(pieces):
+        u = slab if a == slab else -a - n
+        onward.append(
             remote(
-                orb.at[o, pl.ds(jnp.where(left == 1, 0, quarter - n), n)],
-                p0.at[pl.ds(placed(slab, n) + rims[0], n)],
-                far_send.at[o, 4], far_recv.at[4], partners[o],
+                held.at[at, pl.ds(0, n)],
+                p0.at[pl.ds(jnp.where(left == 1, slab - n - u, u) + rims[0], n)],
+                onward_send.at[at], onward_recv.at[at], onward_to,
             )
         )
-        far.append(group)
+
+    def pass_on(*numbers):
+        for at in numbers:
+            far[0][at].wait_recv()
+            onward[at].start()
+
     part = pot_rim // 8
     pot_far = [
         remote(
@@ -312,8 +338,11 @@
     near.wait_recv()
     near_pot.wait_recv()
     apply(0, 8, 4, 12)
+    pass_on(4, 0)
     apply(1, 14, 3, 12)
+    pass_on(1)
     apply(2, 20, 2, 12)
+    pass_on(2)
     spread(20, 24)
 
     pot_far[0].wait_recv()
@@ -330,7 +359,8 @@
     for copy in passed:
         copy.start()
 
-    far[0][4].wait_recv()
+    pass_on(3)
+    onward[4].wait_recv()
     apply(0, slab - 8, 1, 8)
     apply(1, slab - 14, 1, 8)
     apply(2, slab - 20, 1, 8)
@@ -339,7 +369,7 @@
         if at == 1:
             for copy in passed:
                 copy.wait_recv()
-        far[0][at].wait_recv()
+        onward[at].wait_recv()
         advance(-8 * at)
 
     @pl.when(long)
@@ -354,7 +384,7 @@
         for o in range(2):
             far[o][4].wait_send()
 
-    for copy in (near, near_pot, *passed):
+    for copy in (near, near_pot, *passed, *onward):
         copy.wait_send()
     own_rows.wait()
     pltpu.make_async_copy(out.at[0], recv.at[row], move_sem.at[3]).wait()
@@ -410,9 +440,12 @@
             ],
             pltpu.VMEM((2 * (slab + 2 * shift), 8, 128), f32),
             pltpu.VMEM((slab + 2 * (shift + REACH * (DEG - 1)), 2, 8, 128), f32),
+            pltpu.VMEM((5, 8, 2, 8, 128), f32),
             dma((2,)),
             dma((2,)),
             dma((2, 5)),
+            dma((5,)),
+            dma((5,)),
             dma((5,)),
             dma((2,)),
             dma,

time: 42.4 us -> 42.3 us (level)
  no operation moved by 1% of the time
where the time goes in v5:
time: 42.3 us; the launch traced here: 41.9 us
  Pallas kernels  41.9 us (99%)
    pallas_call x1, Pallas kernels, per_device(): pl.pallas_call(functools.partial(filter_kernel, bands), out_shape=(pltpu....  40.6 us
    pallas_call x1, Pallas kernels, per_device(): pl.pallas_call(rotate_kernel, out_shape=jax.ShapeDtypeStruct((bands * orb...  1.31 us

profile of v5, /device:TPU:32, one launch (start us, length us, event | category | flops | bytes accessed | tf_op | source)
XLA Modules:
  0.0 41.9 jit_solution(2667003049440790790)
XLA Ops:
  0.0 40.6 %filter.1 = (f32[128,8,128]{2,1,0:T(8,128)S(1)}, f32[64,2,128]{2,1,0:T(2,128)S(1)}) custom-call(f32[2,32,2,8,128]{4,3,2,1,0:T(8,128)} %bitcast.4, f32[32,2,8,128]{3,2,1,0:T(8,128)} %bitcast.5, f32[2,128]{1,0:T(2,128)} %sub.1), custom_call_target="tpu_custom_call" | custom-call | tf_op jit(solution)/shard_map/filter/pallas_call | solution.py:428
  40.6 1.3 %rotate.1 = f32[128,1024]{1,0:T(8,128)} custom-call(f32[64,2,8,128]{3,2,1,0:T(8,128)S(1)} %bitcast.3, f32[64,2,128]{2,1,0:T(2,128)S(1)} %get-tuple-element.8.rows_v), custom_call_target="tpu_custom_call" | custom-call | tf_op jit(solution)/shard_map/rotate/pallas_call | solution.py:466
